TPU v7x, 256 devices: a whole 4x4x8 slice. The times are simulated.
256 devices in a mesh: seq: 32 (over y, z), mp: 8 (over x, core).
Axes of the slice: x: 4, y: 4, z: 8, core: 2. Of those that a mesh axis runs over, the one named last changes fastest.
Arguments:
- patch_hidden: bfloat16 [16384, 5120], P('seq', 'mp'), may hold values from -6 to 6
- out_weight: bfloat16 [5120, 8192], P(None, 'mp'), may hold values from -0.078125 to 0.078125
- out_bias: bfloat16 [8192], P('mp'), may hold values from -3 to 3
- cluster_ids: int32 [16384], P('seq'), may hold values from 0 to 8191, as said below
- memory_slots: bfloat16 [8192, 8192], P('seq', 'mp'), may hold values from -6 to 6
- slot_counts: int32 [8192], P('seq'), may hold values from 1 to 16
- norm_gain: bfloat16 [8192], P('mp'), may hold values from 0.099609375 to 1.8984375
- key_weight: bfloat16 [8192, 1024], P('seq', 'mp'), may hold values from -0.0625 to 0.0625
- value_weight: bfloat16 [8192, 1024], P('seq', 'mp'), may hold values from -0.0625 to 0.0625
- key_bias: bfloat16 [1024], P('mp'), may hold values from -3 to 3
- value_bias: bfloat16 [1024], P('mp'), may hold values from -3 to 3
Outputs:
- memory_new: bfloat16 [8192, 8192], P('seq', 'mp')
- slot_keys: bfloat16 [8192, 1024], P('seq', 'mp')
- slot_values: bfloat16 [8192, 1024], P('seq', 'mp')
Inputs may be any that keep to these rules, and one draw needn't show every extreme that they name: `cluster_ids`: slots s * 256 to (s + 1) * 256 - 1 belong to index s of seq. Of the 512 rows of one index of seq, at most 48 name slots of any one index of seq, and in every draw some index of seq receives exactly 48 rows from every index of seq.
All inputs are finite; a program needn't handle non-finite values.
Results may differ from a plain program's by a relative error of at most 0.0054.
Values may be sent and summed in bfloat16 or wider, within the bound.
A program may use at most 128 MiB of HBM per device.

v0:
```python
import jax
import jax.numpy as jnp
from jax import lax
from jax.sharding import PartitionSpec as P

D = 8192


def on_device(
    patch_hidden,
    out_weight,
    out_bias,
    cluster_ids,
    memory_slots,
    slot_counts,
    norm_gain,
    key_weight,
    value_weight,
    key_bias,
    value_bias,
):
    row_count = patch_hidden.shape[0]
    width_local = out_weight.shape[1]
    slot_local = memory_slots.shape[0]
    seq_count = lax.axis_size("seq")
    capacity = 3 * row_count // seq_count
    bias_wide = out_bias.astype(jnp.float32)
    owner = cluster_ids // slot_local
    owner_table = (owner[:, None] == jnp.arange(seq_count, dtype=jnp.int32)[None, :]).astype(
        jnp.int32
    )
    rank = jnp.sum(jnp.cumsum(owner_table, axis=0) * owner_table, axis=1) - 1
    target = owner * capacity + rank
    send_slots = (
        jnp.full((seq_count * capacity,), -1, jnp.int32).at[target].set(cluster_ids % slot_local)
    )
    activated = jax.nn.gelu(
        lax.all_gather(patch_hidden, "mp", axis=1, tiled=True).astype(jnp.float32),
        approximate=False,
    ).astype(jnp.bfloat16)
    projected = jnp.dot(activated, out_weight, preferred_element_type=jnp.float32)
    merged = projected + bias_wide[None, :]
    send_rows = jnp.zeros((seq_count * capacity, width_local), jnp.float32).at[target].set(merged)
    got_rows, got_slots = (
        lax.all_to_all(send_rows, "seq", split_axis=0, concat_axis=0, tiled=True),
        lax.all_to_all(send_slots, "seq", split_axis=0, concat_axis=0, tiled=True),
    )
    matches = jnp.arange(slot_local, dtype=jnp.int32)[:, None] == got_slots[None, :]
    totals = jnp.dot(
        matches.astype(jnp.float32),
        got_rows,
        precision=lax.Precision.HIGHEST,
        preferred_element_type=jnp.float32,
    )
    arrivals = jnp.sum(matches.astype(jnp.float32), axis=1)
    weight = slot_counts.astype(jnp.float32)
    memory_new = (
        (weight[:, None] * memory_slots.astype(jnp.float32) + totals) / (weight + arrivals)[:, None]
    ).astype(jnp.bfloat16)
    key_full, value_full = (
        lax.all_gather(key_weight, "seq", axis=0, tiled=True),
        lax.all_gather(value_weight, "seq", axis=0, tiled=True),
    )
    head_local = key_full.shape[1]
    stored = lax.optimization_barrier(memory_new).astype(jnp.float32)
    squares = lax.psum(jnp.sum(stored * stored, axis=1), "mp")
    inverse = lax.rsqrt(squares / D + 1e-06)
    normed = (stored * inverse[:, None] * norm_gain.astype(jnp.float32)[None, :]).astype(
        jnp.bfloat16
    )
    key_rows, value_rows = (
        lax.all_to_all(key_full, "mp", split_axis=0, concat_axis=1, tiled=True),
        lax.all_to_all(value_full, "mp", split_axis=0, concat_axis=1, tiled=True),
    )
    mp_count = key_rows.shape[1] // head_local
    joined = jnp.stack(
        [
            key_rows.reshape(width_local, mp_count, head_local),
            value_rows.reshape(width_local, mp_count, head_local),
        ],
        axis=2,
    ).reshape(width_local, 2 * mp_count * head_local)
    shared = lax.psum_scatter(
        lax.dot_general(
            joined, normed, (((0,), (1,)), ((), ())), preferred_element_type=jnp.float32
        ),
        "mp",
        scatter_dimension=0,
        tiled=True,
    )
    combined = shared.T
    key_part = combined[:, :head_local]
    value_part = combined[:, head_local:]
    slot_keys = (key_part + key_bias.astype(jnp.float32)[None, :]).astype(jnp.bfloat16)
    slot_values = (value_part + value_bias.astype(jnp.float32)[None, :]).astype(jnp.bfloat16)
    return (memory_new, slot_keys, slot_values)


def solution(mesh):
    return jax.shard_map(
        on_device,
        mesh=mesh,
        in_specs=(
            P("seq", "mp"),
            P(None, "mp"),
            P("mp"),
            P("seq"),
            P("seq", "mp"),
            P("seq"),
            P("mp"),
            P("seq", "mp"),
            P("seq", "mp"),
            P("mp"),
            P("mp"),
        ),
        out_specs=(P("seq", "mp"), P("seq", "mp"), P("seq", "mp")),
        check_vma=False,
    )
```

profile of v0, /device:TPU:6, one launch (start us, length us, event | category | flops | bytes accessed | tf_op | source)
XLA Modules:
  0.0 473.9 jit_solution(14380446403744334530)
XLA Ops:
  7.2 0.7 all-gather.8.cloned.1.call-update
  7.9 0.7 all-gather.6.cloned.1.call-update
  8.7 0.7 all-gather.4.cloned.1.call-update
  9.4 0.7 add_select_fusion
  10.1 1.2 reduce-window.6
  11.3 0.2 slice_reduce_fusion
  11.5 0.1 fusion.52
  11.6 2.5 scatter_custom_fusion
  14.2 21.1 %all_to_all.53 = s32[32,48,1]{1,2,0:T(1,128)S(1)} all-to-all(s32[32,48,1]{1,2,0:T(1,128)S(1)} %bitcast.39), channel_id=1, replica_groups=mesh['seq'=32,'mp'=8] {'seq'}, dimensions={0} | all-to-all | bytes 12288 | tf_op jit(solution)/shard_map/all_to_all | solution.py:46
  35.2 56.2 %all-gather.8.cloned.1.call-done = bf16[8192,128]{1,0:T(8,128)(2,1)} async-done(((bf16[256,128]{1,0:T(8,128)(2,1)}), bf16[8192,128]{1,0:T(8,128)(2,1)}) %all-gather.8.cloned.1.call-update) | async-done | bytes 2097168 | tf_op jit(solution)/shard_map/all_gather | solution.py:62
  91.4 4.8 %all-to-all-start.3 = ((bf16[8,1024,128]{2,1,0:T(8,128)(2,1)}), bf16[8,1024,128]{2,1,0:T(8,128)(2,1)S(1)}, u32[]{:S(2)}, u32[]{:S(2)}) async-start(bf16[8,1024,128]{2,1,0:T(8,128)(2,1)} %bitcast.37), calls=%async_computation.3 | async-start | bytes 4194304 | tf_op jit(solution)/shard_map/all_to_all | solution.py:73
  96.2 0.7 convert_element_type.53
  96.9 72.2 %all-gather.6.cloned.1.call-done = bf16[8192,128]{1,0:T(8,128)(2,1)} async-done(((bf16[256,128]{1,0:T(8,128)(2,1)}), bf16[8192,128]{1,0:T(8,128)(2,1)}) %all-gather.6.cloned.1.call-update) | async-done | bytes 2097168 | tf_op jit(solution)/shard_map/all_gather | solution.py:61
  169.2 4.8 %all-to-all-start.2 = ((bf16[8,1024,128]{2,1,0:T(8,128)(2,1)}), bf16[8,1024,128]{2,1,0:T(8,128)(2,1)}, u32[]{:S(2)}, u32[]{:S(2)}) async-start(bf16[8,1024,128]{2,1,0:T(8,128)(2,1)} %bitcast.36), calls=%async_computation.2 | async-start | bytes 4194304 | tf_op jit(solution)/shard_map/all_to_all | solution.py:72
  174.0 47.3 %all-gather.4.cloned.1.call-done = bf16[512,5120]{1,0:T(8,128)(2,1)} async-done(((bf16[512,640]{1,0:T(8,128)(2,1)}), bf16[512,5120]{1,0:T(8,128)(2,1)}) %all-gather.4.cloned.1.call-update) | async-done | bytes 5242896 | tf_op jit(solution)/shard_map/all_gather | solution.py:38
  221.2 31.9 %fusion.31 = f32[512,1024]{1,0:T(8,128)} fusion(bf16[5120,1024]{1,0:T(8,128)(2,1)} %param.12, bf16[512,5120]{1,0:T(8,128)(2,1)} %all-gather.4.cloned.1.call-done), kind=kOutput, calls=%fused_computation.36 | convolution fusion | flops 5541724160 | bytes 17825792 | tf_op jit(solution)/shard_map/dot_general | solution.py:41
  253.1 6.4 %scatter_custom_fusion.1 = f32[1536,1024]{1,0:T(8,128)} fusion(s32[512]{0:T(512)S(1)} %compare_select_fusion, f32[]{:T(128)} %constant.48.clone.1, f32[512,1024]{1,0:T(8,128)} %fusion.31, f32[1024]{0:T(1024)S(1)} %convert_element_type.53), kind=kCustom, calls=%fused_computation.38 | custom fusion | flops 524288 | bytes 8392708 | tf_op jit(solution)/shard_map/scatter | solution.py:43
  259.6 5.9 %all-to-all-start.1 = ((f32[32,48,1024]{2,1,0:T(8,128)}), f32[32,48,1024]{2,1,0:T(8,128)}, u32[]{:S(2)}, u32[]{:S(2)}) async-start(f32[32,48,1024]{2,1,0:T(8,128)} %bitcast.33), calls=%async_computation.1 | async-start | bytes 12582912 | tf_op jit(solution)/shard_map/all_to_all | solution.py:45
  265.6 0.5 broadcast.74
  266.1 0.7 reduce.5
  266.9 0.2 convert_reduce_fusion
  267.1 3.9 pad_maximum_fusion
  271.0 6.5 %copy.30 = bf16[1024,8,2,128]{0,3,2,1:T(8,128)(2,1)} copy(bf16[1024,8,2,128]{3,0,1,2:T(8,128)(2,1)} %pad_maximum_fusion) | data formatting | bytes 8388608 | tf_op jit(solution)/shard_map/stack | solution.py:76
  277.5 129.7 %all-to-all-done.1 = f32[32,48,1024]{2,1,0:T(8,128)} async-done(((f32[32,48,1024]{2,1,0:T(8,128)}), f32[32,48,1024]{2,1,0:T(8,128)}, u32[]{:S(2)}, u32[]{:S(2)}) %all-to-all-start.1) | async-done | bytes 6291488 | tf_op jit(solution)/shard_map/all_to_all | solution.py:45
  407.2 6.3 %fusion.39 = bf16[256,1024]{1,0:T(8,128)(2,1)S(1)} fusion(f32[1536,1024]{1,0:T(8,128)} %bitcast.4, bf16[256,1024]{1,0:T(8,128)(2,1)S(1)} %copy-done.3, s32[1536]{0:T(1024)S(1)} %eq.48, f32[256]{0:T(256)S(1)} %convert_add_fusion, f32[256]{0:T(256)S(1)} %convert_element_type.48), kind=kOutput, calls=%fused_computation.48 | convolution fusion | flops 4833542144 | bytes 7348224 | tf_op jit(solution)/shard_map/dot_general | solution.py:49
  413.5 0.2 fusion.40
  413.7 10.9 %psum.7 = f32[256]{0:T(256)S(1)} all-reduce(f32[256]{0:T(256)S(1)} %fusion.40), channel_id=1, replica_groups=mesh['seq'=32,'mp'=8] {'mp'}, use_global_device_ids=true, to_apply=%region_7.8 | all-reduce | flops 256 | bytes 2048 | tf_op jit(solution)/shard_map/psum | solution.py:66
  424.5 4.9 %fusion.45 = f32[2048,256]{1,0:T(8,128)} fusion(bf16[1024,2048]{0,1:T(8,128)(2,1)} %bitcast.35, bf16[256,1024]{1,0:T(8,128)(2,1)S(1)} %fusion.39, f32[1024]{0:T(1024)S(1)} %convert_element_type.57, f32[256]{0:T(256)S(1)} %add_rsqrt_fusion), kind=kOutput, calls=%fused_computation.54 | convolution fusion | flops 1074790400 | bytes 6820864 | tf_op jit(solution)/shard_map/dot_general | solution.py:84
  429.5 35.3 %reduce-scatter.2.cloned.1.call-done = f32[256,256]{1,0:T(8,128)} async-done(((f32[2048,256]{1,0:T(8,128)}), f32[256,256]{1,0:T(8,128)}) %reduce-scatter.2.cloned.1.call-update) | async-done | bytes 262160 | tf_op jit(solution)/shard_map/reduce_scatter | solution.py:83
  464.8 1.1 fusion.49
  465.9 0.7 copy.31
  466.6 0.7 copy.32
  (31 shorter events, 0.4 us)
Async XLA Ops:
  7.2 84.3 %all-gather.8.cloned.1.call-start = ((), (), s32[]{:S(2)}) async-start(), calls=%async_computation.7 | async-start | bytes 2162688 | tf_op jit(solution)/shard_map/all_gather | solution.py:62
  7.9 161.3 %all-gather.6.cloned.1.call-start = ((), (), s32[]{:S(2)}) async-start(), calls=%async_computation.6 | async-start | bytes 2162688 | tf_op jit(solution)/shard_map/all_gather | solution.py:61
  8.6 212.6 %all-gather.4.cloned.1.call-start = ((), (), s32[]{:S(2)}) async-start(), calls=%async_computation.5 | async-start | bytes 5898240 | tf_op jit(solution)/shard_map/all_gather | solution.py:38
  91.4 77.7 %all-to-all-start.3 = ((bf16[8,1024,128]{2,1,0:T(8,128)(2,1)}), bf16[8,1024,128]{2,1,0:T(8,128)(2,1)S(1)}, u32[]{:S(2)}, u32[]{:S(2)}) async-start(bf16[8,1024,128]{2,1,0:T(8,128)(2,1)} %bitcast.37), calls=%async_computation.3 | async-start | bytes 4194304 | tf_op jit(solution)/shard_map/all_to_all | solution.py:73
  169.2 90.4 %all-to-all-start.2 = ((bf16[8,1024,128]{2,1,0:T(8,128)(2,1)}), bf16[8,1024,128]{2,1,0:T(8,128)(2,1)}, u32[]{:S(2)}, u32[]{:S(2)}) async-start(bf16[8,1024,128]{2,1,0:T(8,128)(2,1)} %bitcast.36), calls=%async_computation.2 | async-start | bytes 4194304 | tf_op jit(solution)/shard_map/all_to_all | solution.py:72
  253.1 12.4 %copy-start.1 = (s32[256]{0:T(256)S(1)}, s32[256]{0:T(256)}, u32[]{:S(2)}) copy-start(s32[256]{0:T(256)} %param.16) | copy-start | bytes 3076
  253.1 12.4 %copy-start.2 = (bf16[1024]{0:T(1024)(128)(2,1)S(1)}, bf16[1024]{0:T(1024)(128)(2,1)}, u32[]{:S(2)}) copy-start(bf16[1024]{0:T(1024)(128)(2,1)} %param.17) | copy-start | bytes 6148
  259.6 147.6 %all-to-all-start.1 = ((f32[32,48,1024]{2,1,0:T(8,128)}), f32[32,48,1024]{2,1,0:T(8,128)}, u32[]{:S(2)}, u32[]{:S(2)}) async-start(f32[32,48,1024]{2,1,0:T(8,128)} %bitcast.33), calls=%async_computation.1 | async-start | bytes 12582912 | tf_op jit(solution)/shard_map/all_to_all | solution.py:45
  265.5 141.7 %copy-start.3 = (bf16[256,1024]{1,0:T(8,128)(2,1)S(1)}, bf16[256,1024]{1,0:T(8,128)(2,1)}, u32[]{:S(2)}) copy-start(bf16[256,1024]{1,0:T(8,128)(2,1)} %param.15) | copy-start | bytes 1572868
  265.5 199.3 %reduce-scatter.2.cloned.1.call-start = ((), (), s32[]{:S(2)}) async-start(), calls=%async_computation.8 | async-start | bytes 2359296 | tf_op jit(solution)/shard_map/reduce_scatter | solution.py:83
  277.5 152.0 %copy-start.4 = (bf16[128]{0:T(256)(128)(2,1)S(1)}, bf16[128]{0:T(256)(128)(2,1)}, u32[]{:S(2)}) copy-start(bf16[128]{0:T(256)(128)(2,1)} %param.21) | copy-start | bytes 772
  277.5 152.0 %copy-start.5 = (bf16[128]{0:T(256)(128)(2,1)S(1)}, bf16[128]{0:T(256)(128)(2,1)}, u32[]{:S(2)}) copy-start(bf16[128]{0:T(256)(128)(2,1)} %param.20) | copy-start | bytes 772
  413.5 53.9 %copy-start = (bf16[256,1024]{1,0:T(8,128)(2,1)}, bf16[256,1024]{1,0:T(8,128)(2,1)S(1)}, u32[]{:S(2)}) copy-start(bf16[256,1024]{1,0:T(8,128)(2,1)S(1)} %fusion.39) | copy-start | bytes 1572868
Sparse Core Ops, SparseCore 0:
  10.6 80.7 all-gather.7
  94.0 75.0 all-gather.5
  171.0 50.1 all-gather.3
  429.6 35.1 reduce-scatter.1
where the time goes:
time: 478 us; the launch traced here: 474 us
  waiting for transfers between devices  343 us (72%)
  matrix products  43.1 us (9%)
  blocking collectives  31.9 us (7%)
  starting transfers between devices  15.6 us (3%)
  other arithmetic  15.2 us (3%)
  between operations  13.9 us (3%)
  local copies, waits for them, and re-layouts  11.3 us (2%)
    all_to_all x1, waiting for transfers between devices, on_device(): lax.all_to_all(send_rows, 'seq', split_axis=0, concat_axis=0, tiled=True)  130 us
    all_gather x1, waiting for transfers between devices, on_device(): lax.all_gather(key_weight, 'seq', axis=0, tiled=True)  72.2 us
    all_gather x1, waiting for transfers between devices, on_device(): lax.all_gather(value_weight, 'seq', axis=0, tiled=True)  56.2 us
    all_gather x1, waiting for transfers between devices, on_device(): lax.all_gather(patch_hidden, 'mp', axis=1, tiled=True).astype(jnp.float32)  47.3 us
    reduce_scatter x1, waiting for transfers between devices, on_device(): lax.psum_scatter(lax.dot_general(joined, normed, (((0,), (1,)), ((), ()))...  35.3 us
    dot_general x1, matrix products, on_device(): jnp.dot(activated, out_weight, preferred_element_type=jnp.float32)  31.9 us
    all_to_all x1, blocking collectives, on_device(): lax.all_to_all(send_slots, 'seq', split_axis=0, concat_axis=0, tiled=True)  21.1 us
    psum x1, blocking collectives, on_device(): squares = lax.psum(jnp.sum(stored * stored, axis=1), 'mp')  10.9 us
  transfers between devices with their start and end apart: 7, of which 5 were waited for; matrix products, arithmetic and copies ran while one was open for 12% of the time, Pallas kernels for 0%

commit v1 on v0

v1 whole, which is shorter than its diff:
```python
import jax
import jax.numpy as jnp
from jax import lax
from jax.experimental import pallas as pl
from jax.experimental.pallas import tpu as pltpu
from jax.sharding import PartitionSpec as P

D = 8192
CHUNKS = ((0, 256), (256, 256), (512, 128))
MESH = pl.DeviceIdType.MESH
N_REMOTE = 110
N_LOCAL = 12
F32, BF16 = jnp.float32, jnp.bfloat16


def gelu(v):
    return v * (1.0 + lax.erf(v * 0.7071067811865476)) * 0.5


def kernel(
    patch,
    wout,
    bias,
    ids,
    mem,
    counts,
    gain,
    kw,
    vw,
    kb,
    vb,
    mem_out,
    key_out,
    val_out,
    pv0,
    pv1,
    pv2,
    h0,
    h1,
    h2,
    idsb,
    oh,
    sp0,
    sp1,
    sp2,
    sm0,
    sm1,
    sm2,
    rp0,
    rp1,
    rp2,
    rm0,
    rm1,
    rm2,
    hs0,
    hs1,
    hs2,
    wv,
    mv,
    acc,
    kvown,
    wkv,
    gbuf,
    mnew,
    ks,
    kr,
    k1s,
    k1r,
    k2s,
    k2r,
    sq,
    kout,
    vout,
    ssem,
    rsem,
    lsem,
):
    pv, h = (pv0, pv1, pv2), (h0, h1, h2)
    sp, sm, rp, rm = (sp0, sp1, sp2), (sm0, sm1, sm2), (rp0, rp1, rp2), (rm0, rm1, rm2)
    hs = (hs0, hs1, hs2)
    seq, mp = lax.axis_index("seq"), lax.axis_index("mp")
    y, z = lax.div(seq, 8), lax.rem(seq, 8)
    x, c = lax.div(mp, 2), lax.rem(mp, 2)

    def m4(v):
        return lax.rem(v + 4, 4)

    def m8(v):
        return lax.rem(v + 8, 8)

    def dev(dy=0, dz=0, dx=0, other=False):
        return (m4(y + dy) * 8 + m8(z + dz), m4(x + dx) * 2 + (1 - c if other else c))

    yp, ym = dev(dy=1), dev(dy=-1)
    zp, zm = dev(dz=1), dev(dz=-1)
    xp, xm = dev(dx=1), dev(dx=-1)
    sib = dev(other=True)
    perm_to = (x * 8 + lax.rem(2 * lax.rem(z, 4) + c + 4, 8), lax.div(seq, 4))
    q = lax.rem(z + 4, 8)
    perm_from = (x * 8 + 4 * c + lax.div(q, 2), 2 * y + lax.rem(q, 2))

    used = [0, 0]
    sends = []

    def remote(src, dst, to, land=None):
        i = used[0]
        used[0] += 1
        copy = pltpu.make_async_remote_copy(
            src_ref=src,
            dst_ref=dst,
            send_sem=ssem.at[i],
            recv_sem=rsem.at[i],
            device_id=to,
            device_id_type=MESH,
        )
        copy.start()
        sends.append(copy)
        if land is None:
            return copy
        return pltpu.make_async_remote_copy(
            src_ref=land,
            dst_ref=land,
            send_sem=ssem.at[i],
            recv_sem=rsem.at[i],
            device_id=to,
            device_id_type=MESH,
        )

    def local(src, dst):
        i = used[1]
        used[1] += 1
        copy = pltpu.make_async_copy(src, dst, lsem.at[i])
        copy.start()
        return copy

    barrier = pltpu.get_barrier_semaphore()
    partners = [yp, ym, zp, zm, perm_to, perm_from, sib]
    partners += [dev(dx=d, other=o) for d in (1, 2, 3) for o in (False, True)]
    for partner in partners:
        pl.semaphore_signal(barrier, inc=1, device_id=partner, device_id_type=MESH)

    got_patch = [local(patch.at[:, pl.ds(o, w)], pv[i]) for i, (o, w) in enumerate(CHUNKS)]
    got_kw = local(kw, kvown.at[:, pl.ds(0, 128)])
    got_vw = local(vw, kvown.at[:, pl.ds(128, 128)])
    got_mem = local(mem, mv)
    got_w = local(wout, wv)

    idsb[0, 0] = ids[...]

    def activate(i):
        got_patch[i].wait()

        def body(r, carry):
            part = pl.ds(pl.multiple_of(r * 64, 64), 64)
            h[i][0, part, :] = gelu(pv[i][part, :].astype(F32)).astype(BF16)
            return carry

        lax.fori_loop(0, 8, body, 0)

    activate(0)
    got_kw.wait()
    got_vw.wait()
    pl.semaphore_wait(barrier, len(partners))

    yc = [{} for _ in CHUNKS]

    def y_first(i):
        yc[i]["p"] = remote(h[i].at[0], h[i].at[1], yp)
        yc[i]["m"] = remote(h[i].at[0], h[i].at[2], ym)

    def y_fwd(i):
        yc[i]["p"].wait_recv()
        yc[i]["fp"] = remote(h[i].at[1, pl.ds(0, 256)], h[i].at[3, pl.ds(0, 256)], yp)
        yc[i]["m"].wait_recv()
        yc[i]["fm"] = remote(h[i].at[2, pl.ds(256, 256)], h[i].at[3, pl.ds(256, 256)], ym)

    def y_done(i):
        yc[i]["fp"].wait_recv()
        yc[i]["fm"].wait_recv()

    wc = {}

    def w_perm():
        wc["perm"] = remote(kvown, wkv.at[perm_to_y, perm_to_z], perm_to, land=wkv.at[y, z])

    perm_to_y = x
    perm_to_z = lax.rem(2 * lax.rem(z, 4) + c + 4, 8)

    def w_z(t):
        if t == 1:
            wc["perm"].wait_recv()
        else:
            wc["zp", t - 1].wait_recv()
            wc["zm", t - 1].wait_recv()
        if t <= 3:
            a, b = m8(z - t + 1), m8(z + t - 1)
            wc["zp", t] = remote(wkv.at[y, a], wkv.at[y, a], zp, land=wkv.at[y, m8(z - t)])
            wc["zm", t] = remote(wkv.at[y, b], wkv.at[y, b], zm, land=wkv.at[y, m8(z + t)])
        else:
            a, b, f = m8(z - 3), m8(z + 3), m8(z + 4)
            lo, hi = pl.ds(0, 128), pl.ds(128, 128)
            wc["zp", 4] = remote(wkv.at[y, a, lo], wkv.at[y, a, lo], zp, land=wkv.at[y, f, lo])
            wc["zm", 4] = remote(wkv.at[y, b, hi], wkv.at[y, b, hi], zm, land=wkv.at[y, f, hi])

    def w_y(t):
        if t == 1:
            wc["zp", 4].wait_recv()
            wc["zm", 4].wait_recv()
            wc["yp"] = remote(wkv.at[y], wkv.at[y], yp, land=wkv.at[m4(y - 1)])
            wc["ym"] = remote(wkv.at[y], wkv.at[y], ym, land=wkv.at[m4(y + 1)])
        else:
            a, b, f = m4(y - 1), m4(y + 1), m4(y + 2)
            lo, hi = pl.ds(0, 4), pl.ds(4, 4)
            wc["yp"].wait_recv()
            wc["fp"] = remote(wkv.at[a, lo], wkv.at[a, lo], yp, land=wkv.at[f, lo])
            wc["ym"].wait_recv()
            wc["fm"] = remote(wkv.at[b, hi], wkv.at[b, hi], ym, land=wkv.at[f, hi])

    def w_done():
        wc["fp"].wait_recv()
        wc["fm"].wait_recv()

    ic = {}

    def i_first():
        ic["p"] = remote(idsb.at[0, 0], idsb.at[0, 1], yp)
        ic["m"] = remote(idsb.at[0, 0], idsb.at[0, 2], ym)

    def i_fwd():
        ic["p"].wait_recv()
        ic["f"] = remote(idsb.at[0, 1], idsb.at[0, 3], yp)

    def i_z(t):
        if t == 1:
            ic["m"].wait_recv()
            ic["f"].wait_recv()
            ic["zp", 1] = remote(idsb.at[0], idsb.at[1], zp)
            ic["zm", 1] = remote(idsb.at[0], idsb.at[5], zm)
        else:
            ic["zp", t - 1].wait_recv()
            ic["zp", t] = remote(idsb.at[t - 1], idsb.at[t], zp)
            if t <= 3:
                ic["zm", t - 1].wait_recv()
                ic["zm", t] = remote(idsb.at[3 + t], idsb.at[4 + t], zm)

    def i_done():
        ic["zp", 4].wait_recv()
        ic["zm", 3].wait_recv()

    def onehot(lo, hi):
        def body(k, carry):
            step = lax.div(k + 1, 2)
            zrel = 4 + step * (1 - 2 * lax.rem(k, 2))
            base = (y * 8 + m8(z + zrel)) * 256
            slot = lax.broadcasted_iota(jnp.int32, (256, 128), 0)
            for s in range(4):
                block = idsb[0, s]
                for r in range(4):
                    row = block[r : r + 1, :] - base
                    hit = jnp.where(slot == row, 1.0, 0.0).astype(BF16)
                    oh[k, :, s * 512 + r * 128 : s * 512 + (r + 1) * 128] = hit
            return carry

        lax.fori_loop(lo, hi, body, 0)

    def sums(i, k, n):
        w = CHUNKS[i][1]
        left = oh[k : k + n].reshape(n * 256, 2048)
        return jnp.dot(left, h[i][...].reshape(2048, w), preferred_element_type=F32)

    rc = [{} for _ in CHUNKS]
    lo, hi = pl.ds(0, 128), pl.ds(128, 128)

    def rs(i, t):
        if t == 0:
            p = sums(i, 0, 1).astype(BF16)
            sp[i][0, lo] = p[:128]
            sm[i][0, hi] = p[128:]
            rc[i]["p", 0] = remote(sp[i].at[0, lo], rp[i].at[0, lo], zp)
            rc[i]["m", 0] = remote(sm[i].at[0, hi], rm[i].at[0, hi], zm)
            return
        p = sums(i, 2 * t - 1, 2)
        rc[i]["p", t - 1].wait_recv()
        if t == 1:
            sp[i][t, lo] = (p[:128] + rp[i][0, lo].astype(F32)).astype(BF16)
            sp[i][t, hi] = p[128:256].astype(BF16)
        else:
            sp[i][t] = (p[:256] + rp[i][t - 1].astype(F32)).astype(BF16)
        rc[i]["p", t] = remote(sp[i].at[t], rp[i].at[t], zp)
        rc[i]["m", t - 1].wait_recv()
        if t == 1:
            sm[i][t, lo] = p[256:384].astype(BF16)
            sm[i][t, hi] = (p[384:] + rm[i][0, hi].astype(F32)).astype(BF16)
        else:
            sm[i][t] = (p[256:] + rm[i][t - 1].astype(F32)).astype(BF16)
        rc[i]["m", t] = remote(sm[i].at[t], rm[i].at[t], zm)

    xc = [{} for _ in CHUNKS]

    def rs_end(i):
        p = sums(i, 7, 1)
        rc[i]["p", 3].wait_recv()
        rc[i]["m", 3].wait_recv()
        hs[i][0] = (p + rp[i][3].astype(F32) + rm[i][3].astype(F32)).astype(BF16)
        xc[i][2] = remote(hs[i].at[0], hs[i].at[2], xp)
        xc[i][4] = remote(hs[i].at[0], hs[i].at[4], xm)
        xc[i][1] = remote(hs[i].at[0], hs[i].at[1], sib)

    def x_fwd(i):
        xc[i][2].wait_recv()
        xc[i]["fp"] = remote(hs[i].at[2, lo], hs[i].at[6, lo], xp)
        xc[i][3] = remote(hs[i].at[2], hs[i].at[3], sib)
        xc[i][4].wait_recv()
        xc[i]["fm"] = remote(hs[i].at[4, hi], hs[i].at[6, hi], xm)
        xc[i][5] = remote(hs[i].at[4], hs[i].at[5], sib)

    def x_last(i):
        xc[i]["fp"].wait_recv()
        xc[i]["fm"].wait_recv()
        xc[i][7] = remote(hs[i].at[6], hs[i].at[7], sib)

    def mm(i, blocks, first=False):
        off, w = CHUNKS[i]
        for b in blocks:
            if b % 2:
                xc[i][b].wait_recv()
            xs = m4(x + (0, -1, 1, 2)[b // 2])
            src = xs * 2 + (1 - c if b % 2 else c)
            got = jnp.dot(hs[i][b], wv[src, off : off + w, :], preferred_element_type=F32)
            acc[...] = got if first and b == blocks[0] else acc[...] + got

    y_first(0)
    w_perm()
    i_first()
    activate(1)
    i_fwd()
    activate(2)
    w_z(1)
    i_z(1)
    onehot(0, 3)
    y_fwd(0)
    y_first(1)
    w_z(2)
    i_z(2)
    onehot(3, 8)
    w_z(3)
    i_z(3)
    y_done(0)
    rs(0, 0)
    w_z(4)
    i_z(4)
    rs(0, 1)
    y_fwd(1)
    y_first(2)
    rs(0, 2)
    y_done(1)
    rs(1, 0)
    rs(0, 3)
    rs(1, 1)
    y_fwd(2)
    w_y(1)
    rs_end(0)
    rs(1, 2)
    y_done(2)
    rs(2, 0)
    x_fwd(0)
    rs(1, 3)
    got_w.wait()
    mm(0, (0, 1), first=True)
    rs(2, 1)
    x_last(0)
    rs_end(1)
    rs(2, 2)
    mm(0, (2, 3, 4, 5))
    rs(2, 3)
    x_fwd(1)

    i_done()
    own = seq * 256

    def count(p, carry):
        slot = lax.broadcasted_iota(jnp.int32, (256, 128), 0) + own
        for s in range(4):
            block = idsb[p, s]
            for r in range(4):
                carry = carry + jnp.where(slot == block[r : r + 1, :], 1.0, 0.0)
        return carry

    hits = lax.fori_loop(0, 8, count, jnp.zeros((256, 128), F32))
    arrivals = jnp.broadcast_to(jnp.sum(hits, axis=1, keepdims=True), (256, 128))
    weight = jnp.transpose(jnp.broadcast_to(counts[...].astype(F32), (128, 256)))
    share = 1.0 / (weight + arrivals)

    mm(0, (6, 7))
    rs_end(2)
    x_last(1)
    mm(1, (0, 1, 2, 3, 4, 5))
    x_fwd(2)
    mm(2, (0, 1))
    mm(1, (6, 7))
    x_last(2)
    mm(2, (2, 3, 4, 5))
    w_y(2)
    mm(2, (6, 7))

    got_mem.wait()
    squares = jnp.zeros((256, 128), F32)
    for j in range(8):
        col = slice(j * 128, (j + 1) * 128)
        b = bias[:, col].astype(F32)
        total = acc[:, col] + arrivals * b
        new = ((weight * mv[:, col].astype(F32) + total) * share).astype(BF16)
        mnew[:, col] = new
        stored = new.astype(F32)
        squares = squares + stored * stored
        gbuf[:, col] = (stored * gain[:, col].astype(F32)).astype(BF16)
    put_mem = local(mnew, mem_out)
    mine = jnp.broadcast_to(jnp.sum(squares, axis=1, keepdims=True), (256, 128))
    sq[0] = jnp.transpose(mine)[:8, :]
    sqc = []
    for d in (0, 1, 2, 3):
        for o in (False, True):
            if d or o:
                slot = 2 * d + o
                sqc.append(remote(sq.at[0], sq.at[slot], dev(dx=d, other=o)))

    w_done()

    def heads(d, o):
        ys = m4(x + d)
        core = 1 - c if o else c
        total = None
        for r in range(4):
            zs = lax.rem(2 * r + core + 4, 8)
            part = jnp.dot(
                gbuf[:, r * 256 : (r + 1) * 256], wkv[ys, zs], preferred_element_type=F32
            )
            total = part if total is None else total + part
        return total

    kc = {}
    for d in (2, 1, 3, 0):
        ks[d] = heads(d, True).astype(BF16)
        kc[d] = remote(ks.at[d], kr.at[d], sib)
    p = heads(2, False)
    kc[2].wait_recv()
    p = (p + kr[2].astype(F32)).astype(BF16)
    k1s[...] = p
    kc["p1"] = remote(k1s.at[lo], k1r.at[lo], xp)
    kc["m1"] = remote(k1s.at[hi], k1r.at[hi], xm)
    for d, half, key, to in ((1, 0, "p", xp), (3, 1, "m", xm)):
        p = heads(d, False)
        kc[d].wait_recv()
        p = p + kr[d].astype(F32)
        kc[key + "1"].wait_recv()
        if half == 0:
            k2s[half, lo] = (p[:128] + k1r[lo].astype(F32)).astype(BF16)
            k2s[half, hi] = p[128:].astype(BF16)
        else:
            k2s[half, lo] = p[:128].astype(BF16)
            k2s[half, hi] = (p[128:] + k1r[hi].astype(F32)).astype(BF16)
        kc[key + "2"] = remote(k2s.at[half], k2r.at[half], to)
    p = heads(0, False)
    kc[0].wait_recv()
    p = p + kr[0].astype(F32)
    for copy in sqc:
        copy.wait_recv()
    whole = sq[0]
    for j in range(1, 8):
        whole = whole + sq[j]
    inverse = lax.rsqrt(whole[:1, :] * (1.0 / D) + 1e-06)
    inverse = jnp.transpose(jnp.broadcast_to(inverse, (128, 256)))
    kc["p2"].wait_recv()
    kc["m2"].wait_recv()
    p = p + k2r[0].astype(F32) + k2r[1].astype(F32)
    kout[...] = (p[:, :128] * inverse + kb[...].astype(F32)).astype(BF16)
    vout[...] = (p[:, 128:] * inverse + vb[...].astype(F32)).astype(BF16)
    put_key = local(kout, key_out)
    put_val = local(vout, val_out)
    for copy in sends:
        copy.wait_send()
    put_mem.wait()
    put_key.wait()
    put_val.wait()


def on_device(patch, wout, bias, ids, mem, counts, gain, kw, vw, kb, vb):
    any_, vmem = pl.BlockSpec(memory_space=pl.ANY), pl.BlockSpec(memory_space=pltpu.VMEM)

    def per_chunk(*shape):
        return [pltpu.VMEM((*shape, w), BF16) for _, w in CHUNKS]

    scratch = [
        *per_chunk(512),
        *per_chunk(4, 512),
        pltpu.VMEM((8, 4, 4, 128), jnp.int32),
        pltpu.VMEM((8, 256, 2048), BF16),
        *per_chunk(4, 256),
        *per_chunk(4, 256),
        *per_chunk(4, 256),
        *per_chunk(4, 256),
        *per_chunk(8, 256),
        pltpu.VMEM((8, 640, 1024), BF16),
        pltpu.VMEM((256, 1024), BF16),
        pltpu.VMEM((256, 1024), F32),
        pltpu.VMEM((256, 256), BF16),
        pltpu.VMEM((4, 8, 256, 256), BF16),
        pltpu.VMEM((256, 1024), BF16),
        pltpu.VMEM((256, 1024), BF16),
        pltpu.VMEM((4, 256, 256), BF16),
        pltpu.VMEM((4, 256, 256), BF16),
        pltpu.VMEM((256, 256), BF16),
        pltpu.VMEM((256, 256), BF16),
        pltpu.VMEM((2, 256, 256), BF16),
        pltpu.VMEM((2, 256, 256), BF16),
        pltpu.VMEM((8, 8, 256), F32),
        pltpu.VMEM((256, 128), BF16),
        pltpu.VMEM((256, 128), BF16),
        pltpu.SemaphoreType.DMA((N_REMOTE,)),
        pltpu.SemaphoreType.DMA((N_REMOTE,)),
        pltpu.SemaphoreType.DMA((N_LOCAL,)),
    ]
    return pl.pallas_call(
        kernel,
        out_shape=(
            jax.ShapeDtypeStruct((256, 1024), BF16),
            jax.ShapeDtypeStruct((256, 128), BF16),
            jax.ShapeDtypeStruct((256, 128), BF16),
        ),
        in_specs=[any_, any_, vmem, vmem, any_, vmem, vmem, any_, any_, vmem, vmem],
        out_specs=(any_, any_, any_),
        scratch_shapes=scratch,
        compiler_params=pltpu.CompilerParams(
            collective_id=0, has_side_effects=True, vmem_limit_bytes=58 * 2**20
        ),
        cost_estimate=pl.CostEstimate(
            flops=10_000_000_000, bytes_accessed=20_000_000, transcendentals=330_000
        ),
    )(
        patch,
        wout.reshape(8, 640, 1024),
        bias.reshape(1, 1024),
        ids.reshape(4, 128),
        mem,
        counts.reshape(1, 256),
        gain.reshape(1, 1024),
        kw,
        vw,
        kb.reshape(1, 128),
        vb.reshape(1, 128),
    )


def solution(mesh):
    return jax.shard_map(
        on_device,
        mesh=mesh,
        in_specs=(
            P("seq", "mp"),
            P(None, "mp"),
            P("mp"),
            P("seq"),
            P("seq", "mp"),
            P("seq"),
            P("mp"),
            P("seq", "mp"),
            P("seq", "mp"),
            P("mp"),
            P("mp"),
        ),
        out_specs=(P("seq", "mp"), P("seq", "mp"), P("seq", "mp")),
        check_vma=False,
    )
```

time: 478 us -> 118 us (0.25)
  waiting for transfers between devices: 343 us -> 0 us
  Pallas kernels: 0 us -> 110 us
  matrix products: 43.1 us -> 0 us
  blocking collectives: 31.9 us -> 0 us
  starting transfers between devices: 15.6 us -> 0 us
  other arithmetic: 15.2 us -> 0 us
  between operations: 13.9 us -> 0.64 us
    all_gather x3 -> x0, waiting for transfers between devices: 176 us -> none  [the longest x1 72.2 us: on_device(): lax.all_gather(key_weight, 'seq', axis=0, tiled=True)]
    all_to_all x3 -> x0, waiting for transfers between devices: 130 us -> none  [the longest x1 130 us: on_device(): lax.all_to_all(send_rows, 'seq', split_axis=0, concat_axis=0, tiled=True)]
    pallas_call x0 -> x1, Pallas kernels: none -> 110 us  [on_device(): pl.pallas_call(kernel, out_shape=(jax.ShapeDtypeStruct((256, 1024), BF16)...]
    dot_general x3 -> x0, matrix products: 43.1 us -> none  [the longest x1 31.9 us: on_device(): jnp.dot(activated, out_weight, preferred_element_type=jnp.float32)]
    reduce_scatter x1 -> x0, waiting for transfers between devices: 35.3 us -> none  [on_device(): lax.psum_scatter(lax.dot_general(joined, normed, (((0,), (1,)), ((), ()))...]
    all_to_all x1 -> x0, blocking collectives: 21.1 us -> none  [on_device(): lax.all_to_all(send_slots, 'seq', split_axis=0, concat_axis=0, tiled=True)]
    all_to_all x3 -> x0, starting transfers between devices: 15.5 us -> none  [the longest x1 5.89 us: on_device(): lax.all_to_all(send_rows, 'seq', split_axis=0, concat_axis=0, tiled=True)]
    psum x1 -> x0, blocking collectives: 10.9 us -> none  [on_device(): squares = lax.psum(jnp.sum(stored * stored, axis=1), 'mp')]
  transfers between devices with their start and end apart: 7 -> 0, of which waited for: 5 -> 0; matrix products, arithmetic and copies ran while one was open for 12% -> 0% of each run, Pallas kernels for 0% -> 0%
where the time goes in v1:
time: 118 us
  Pallas kernels  110 us (93%)
  local copies, waits for them, and re-layouts  7.37 us (6%)
    pallas_call x1, Pallas kernels, on_device(): pl.pallas_call(kernel, out_shape=(jax.ShapeDtypeStruct((256, 1024), BF16)...  110 us
    unnamed x3, local copies, waits for them, and re-layouts  4.81 us

profile of v1, /device:TPU:6, one launch (start us, length us, event | category | flops | bytes accessed | tf_op | source)
XLA Modules:
  0.0 118.2 jit_solution(8952178836091768422)
XLA Ops:
  0.6 1.3 %reshape.28.bias = bf16[1,1024]{1,0:T(2,128)(2,1)} reshape(bf16[1024]{0:T(1024)(128)(2,1)} %param.13) | data formatting | bytes 4096 | tf_op jit(solution)/shard_map/reshape | solution.py:542
  1.9 1.3 %reshape.31.gain = bf16[1,1024]{1,0:T(2,128)(2,1)} reshape(bf16[1024]{0:T(1024)(128)(2,1)} %param.17) | data formatting | bytes 4096 | tf_op jit(solution)/shard_map/reshape | solution.py:546
  3.2 110.2 %shard_map.130 = (bf16[256,1024]{1,0:T(8,128)(2,1)}, bf16[256,128]{1,0:T(8,128)(2,1)}, bf16[256,128]{1,0:T(8,128)(2,1)}) custom-call(bf16[512,640]{1,0:T(8,128)(2,1)} %patch.1, bf16[8,640,1024]{2,1,0:T(8,128)(2,1)} %bitcast.5, bf16[1,1024]{1,0:T(2,128)(2,1)} %reshape.28.bias, s32[4,128]{1,0:T(4,128)} %bitcast.6, bf16[256,1024]{1,0:T(8,128)(2,1)} %mem.1, ...), custom_call_target="tpu_custom_call" | custom-call | flops 10000000000 | bytes 20000000 | tf_op jit(solution)/shard_map/pallas_call | solution.py:523
  113.4 1.9 %copy.17 = bf16[256,1024]{1,0:T(8,128)(2,1)} copy(bf16[256,1024]{1,0:T(8,128)(2,1)} %get-tuple-element.6) | data formatting | bytes 1048576
  115.2 1.5 %copy.18 = bf16[256,128]{1,0:T(8,128)(2,1)} copy(bf16[256,128]{1,0:T(8,128)(2,1)} %get-tuple-element.7) | data formatting | bytes 131072
  116.7 1.5 %copy.19 = bf16[256,128]{1,0:T(8,128)(2,1)} copy(bf16[256,128]{1,0:T(8,128)(2,1)} %get-tuple-element.8) | data formatting | bytes 131072

commit v2 on v1

--- a/solution.py
+++ b/solution.py
@@ -329,52 +329,49 @@
             got = jnp.dot(hs[i][b], wv[src, off : off + w, :], preferred_element_type=F32)
             acc[...] = got if first and b == blocks[0] else acc[...] + got
 
+    w_perm()
     y_first(0)
-    w_perm()
+    activate(1)
+    w_z(1)
     i_first()
-    activate(1)
+    y_first(1)
     i_fwd()
+    w_z(2)
     activate(2)
-    w_z(1)
+    y_fwd(0)
+    y_first(2)
+    w_z(3)
     i_z(1)
-    onehot(0, 3)
-    y_fwd(0)
-    y_first(1)
-    w_z(2)
-    i_z(2)
-    onehot(3, 8)
-    w_z(3)
-    i_z(3)
+    onehot(0, 1)
+    onehot(1, 8)
+    y_fwd(1)
+    w_z(4)
     y_done(0)
     rs(0, 0)
-    w_z(4)
-    i_z(4)
-    rs(0, 1)
-    y_fwd(1)
-    y_first(2)
-    rs(0, 2)
+    y_fwd(2)
+    w_y(1)
     y_done(1)
     rs(1, 0)
-    rs(0, 3)
+    rs(0, 1)
     rs(1, 1)
-    y_fwd(2)
-    w_y(1)
-    rs_end(0)
-    rs(1, 2)
+    rs(0, 2)
     y_done(2)
     rs(2, 0)
-    x_fwd(0)
+    rs(1, 2)
+    rs(2, 1)
+    rs(0, 3)
+    i_z(2)
+    rs(2, 2)
     rs(1, 3)
+    rs_end(0)
     got_w.wait()
     mm(0, (0, 1), first=True)
-    rs(2, 1)
-    x_last(0)
+    i_z(3)
+    rs(2, 3)
+    w_y(2)
     rs_end(1)
-    rs(2, 2)
-    mm(0, (2, 3, 4, 5))
-    rs(2, 3)
-    x_fwd(1)
-
+    i_z(4)
+    rs_end(2)
     i_done()
     own = seq * 256
 
@@ -390,30 +387,35 @@
     arrivals = jnp.broadcast_to(jnp.sum(hits, axis=1, keepdims=True), (256, 128))
     weight = jnp.transpose(jnp.broadcast_to(counts[...].astype(F32), (128, 256)))
     share = 1.0 / (weight + arrivals)
-
-    mm(0, (6, 7))
-    rs_end(2)
-    x_last(1)
-    mm(1, (0, 1, 2, 3, 4, 5))
+    x_fwd(0)
+    x_fwd(1)
+    mm(1, (2, 3))
     x_fwd(2)
     mm(2, (0, 1))
+    mm(2, (2, 3))
+    mm(0, (2, 3))
+    mm(1, (4, 5))
+    mm(2, (4, 5))
+    mm(0, (4, 5))
+    x_last(0)
+    mm(1, (0, 1))
+    x_last(1)
+    x_last(2)
+    mm(0, (6, 7))
     mm(1, (6, 7))
-    x_last(2)
-    mm(2, (2, 3, 4, 5))
-    w_y(2)
     mm(2, (6, 7))
 
     got_mem.wait()
     squares = jnp.zeros((256, 128), F32)
     for j in range(8):
         col = slice(j * 128, (j + 1) * 128)
-        b = bias[:, col].astype(F32)
+        b = bias[j : j + 1, :].astype(F32)
         total = acc[:, col] + arrivals * b
         new = ((weight * mv[:, col].astype(F32) + total) * share).astype(BF16)
         mnew[:, col] = new
         stored = new.astype(F32)
         squares = squares + stored * stored
-        gbuf[:, col] = (stored * gain[:, col].astype(F32)).astype(BF16)
+        gbuf[:, col] = (stored * gain[j : j + 1, :].astype(F32)).astype(BF16)
     put_mem = local(mnew, mem_out)
     mine = jnp.broadcast_to(jnp.sum(squares, axis=1, keepdims=True), (256, 128))
     sq[0] = jnp.transpose(mine)[:8, :]
@@ -482,6 +484,16 @@
     put_mem.wait()
     put_key.wait()
     put_val.wait()
+
+
+def hand_over(a, b, c, x, y, z, sem):
+    copies = [
+        pltpu.make_async_copy(s, d, sem.at[i]) for i, (s, d) in enumerate(((a, x), (b, y), (c, z)))
+    ]
+    for copy in copies:
+        copy.start()
+    for copy in copies:
+        copy.wait()
 
 
 def on_device(patch, wout, bias, ids, mem, counts, gain, kw, vw, kb, vb):
@@ -520,7 +532,7 @@
         pltpu.SemaphoreType.DMA((N_REMOTE,)),
         pltpu.SemaphoreType.DMA((N_LOCAL,)),
     ]
-    return pl.pallas_call(
+    made = pl.pallas_call(
         kernel,
         out_shape=(
             jax.ShapeDtypeStruct((256, 1024), BF16),
@@ -539,16 +551,23 @@
     )(
         patch,
         wout.reshape(8, 640, 1024),
-        bias.reshape(1, 1024),
+        bias.reshape(8, 128),
         ids.reshape(4, 128),
         mem,
         counts.reshape(1, 256),
-        gain.reshape(1, 1024),
+        gain.reshape(8, 128),
         kw,
         vw,
         kb.reshape(1, 128),
         vb.reshape(1, 128),
     )
+    return pl.pallas_call(
+        hand_over,
+        out_shape=tuple(jax.ShapeDtypeStruct(m.shape, m.dtype) for m in made),
+        in_specs=[any_, any_, any_],
+        out_specs=(vmem, vmem, vmem),
+        scratch_shapes=[pltpu.SemaphoreType.DMA((3,))],
+    )(*made)
 
 
 def solution(mesh):

time: 118 us -> 96.7 us (0.82); the launches traced: 118 us -> 95.3 us
  Pallas kernels: 110 us -> 94.5 us
  local copies, waits for them, and re-layouts: 7.37 us -> 0 us
    pallas_call x1, Pallas kernels: 110 us -> 92.6 us  [on_device(): pl.pallas_call(kernel, out_shape=(jax.ShapeDtypeStruct((256, 1024), BF16)...]
    unnamed x3 -> x0, local copies, waits for them, and re-layouts: 4.81 us -> none
    reshape x2 -> x0, local copies, waits for them, and re-layouts: 2.56 us -> none  [the longest x1 1.28 us: on_device(): bias.reshape(1, 1024)]
    pallas_call x0 -> x1, Pallas kernels: none -> 1.9 us  [on_device(): pl.pallas_call(hand_over, out_shape=tuple((jax.ShapeDtypeStruct(m.shape,...]
where the time goes in v2:
time: 96.7 us; the launch traced here: 95.3 us
  Pallas kernels  94.5 us (98%)
    pallas_call x1, Pallas kernels, on_device(): pl.pallas_call(kernel, out_shape=(jax.ShapeDtypeStruct((256, 1024), BF16)...  92.6 us

profile of v2, /device:TPU:6, one launch (start us, length us, event | category | flops | bytes accessed | tf_op | source)
XLA Modules:
  0.0 95.3 jit_solution(10020354156467556649)
XLA Ops:
  0.6 92.6 %shard_map.130 = (bf16[256,1024]{1,0:T(8,128)(2,1)}, bf16[256,128]{1,0:T(8,128)(2,1)}, bf16[256,128]{1,0:T(8,128)(2,1)}) custom-call(bf16[512,640]{1,0:T(8,128)(2,1)} %patch.1, bf16[8,640,1024]{2,1,0:T(8,128)(2,1)} %bitcast.7, bf16[8,128]{1,0:T(8,128)(2,1)} %bitcast.8, s32[4,128]{1,0:T(4,128)} %bitcast.9, bf16[256,1024]{1,0:T(8,128)(2,1)} %mem.1, ...), custom_call_target="tpu_custom_call" | custom-call | flops 10000000000 | bytes 20000000 | tf_op jit(solution)/shard_map/pallas_call | solution.py:535
  93.3 1.9 %shard_map.131 = (bf16[256,1024]{1,0:T(8,128)(2,1)}, bf16[256,128]{1,0:T(8,128)(2,1)}, bf16[256,128]{1,0:T(8,128)(2,1)}) custom-call(bf16[256,1024]{1,0:T(8,128)(2,1)} %get-tuple-element.6.a, bf16[256,128]{1,0:T(8,128)(2,1)} %get-tuple-element.7.b, bf16[256,128]{1,0:T(8,128)(2,1)} %get-tuple-element.8.c), custom_call_target="tpu_custom_call" | custom-call | tf_op jit(solution)/shard_map/pallas_call | solution.py:564

commit v3 on v2

--- a/solution.py
+++ b/solution.py
@@ -7,77 +7,116 @@
 
 D = 8192
 CHUNKS = ((0, 256), (256, 256), (512, 128))
+GROUPS = ((0,), (1,), (2,))
+ROWS_B = 32
 MESH = pl.DeviceIdType.MESH
-N_REMOTE = 110
+N_REMOTE = 160
 N_LOCAL = 12
 F32, BF16 = jnp.float32, jnp.bfloat16
 
+ORDER = (
+    ("w_perm",),
+    ("i_first",),
+    ("y_first", 0),
+    ("i_fwd",),
+    ("act", 1),
+    ("w_z", 1, 0),
+    ("y_first", 1),
+    ("w_z", 1, 1),
+    ("oh", 0),
+    ("y_fwd", 0, 1),
+    ("i_z", 1),
+    ("w_z", 2, 1),
+    ("y_fwd", 0, 0),
+    ("w_z", 2, 0),
+    ("oh", 1),
+    ("act", 2),
+    ("i_z", 2),
+    ("w_z", 3, 0),
+    ("y_fwd", 1, 1),
+    ("y_fwd", 1, 0),
+    ("w_z", 3, 1),
+    ("y_first", 2),
+    ("rs", 0, 0),
+    ("w_z", 4, 0),
+    ("i_z", 3),
+    ("w_z", 4, 1),
+    ("b_y", 1, 1),
+    ("rs", 1, 0),
+    ("b_y", 1, 0),
+    ("rs", 0, 1),
+    ("y_fwd", 2, 1),
+    ("y_fwd", 2, 0),
+    ("i_z", 4),
+    ("b_y", 2, 0),
+    ("w_y", 1, 0),
+    ("b_y", 2, 1),
+    ("w_y", 1, 1),
+    ("rs", 1, 1),
+    ("rs", 2, 0),
+    ("rs", 0, 2),
+    ("rs", 2, 1),
+    ("rs", 1, 2),
+    ("rs", 0, 3),
+    ("rs", 2, 2),
+    ("rs", 1, 3),
+    ("b_z", 1, 1),
+    ("count",),
+    ("b_z", 1, 0),
+    ("rs_end", 0),
+    ("rs", 2, 3),
+    ("rs_end", 1),
+    ("b_z", 2, 1),
+    ("w_y", 2, 1),
+    ("w_y", 2, 0),
+    ("b_z", 2, 0),
+    ("rs_end", 2),
+    ("x_fwd", 0, 0),
+    ("x_fwd", 0, 1),
+    ("x_fwd", 1, 1),
+    ("x_fwd", 1, 0),
+    ("mm", 0, 1),
+    ("mm", 0, 0),
+    ("b_z", 3, 0),
+    ("mm", 0, 2),
+    ("b_z", 3, 1),
+    ("x_fwd", 2, 1),
+    ("mm", 1, 2),
+    ("mm", 1, 1),
+    ("mm", 2, 0),
+    ("x_fwd", 2, 0),
+    ("mm", 2, 2),
+    ("mm", 1, 0),
+    ("x_last", 0),
+    ("b_z", 4, 0),
+    ("x_last", 1),
+    ("mm", 0, 3),
+    ("b_z", 4, 1),
+    ("mm", 1, 3),
+    ("x_last", 2),
+    ("mm", 2, 1),
+    ("mm", 2, 3),
+)
+
 
 def gelu(v):
     return v * (1.0 + lax.erf(v * 0.7071067811865476)) * 0.5
 
 
-def kernel(
-    patch,
-    wout,
-    bias,
-    ids,
-    mem,
-    counts,
-    gain,
-    kw,
-    vw,
-    kb,
-    vb,
-    mem_out,
-    key_out,
-    val_out,
-    pv0,
-    pv1,
-    pv2,
-    h0,
-    h1,
-    h2,
-    idsb,
-    oh,
-    sp0,
-    sp1,
-    sp2,
-    sm0,
-    sm1,
-    sm2,
-    rp0,
-    rp1,
-    rp2,
-    rm0,
-    rm1,
-    rm2,
-    hs0,
-    hs1,
-    hs2,
-    wv,
-    mv,
-    acc,
-    kvown,
-    wkv,
-    gbuf,
-    mnew,
-    ks,
-    kr,
-    k1s,
-    k1r,
-    k2s,
-    k2r,
-    sq,
-    kout,
-    vout,
-    ssem,
-    rsem,
-    lsem,
-):
-    pv, h = (pv0, pv1, pv2), (h0, h1, h2)
-    sp, sm, rp, rm = (sp0, sp1, sp2), (sm0, sm1, sm2), (rp0, rp1, rp2), (rm0, rm1, rm2)
-    hs = (hs0, hs1, hs2)
+def kernel(*refs):
+    n = len(CHUNKS)
+    it = iter(refs)
+
+    def take(k):
+        return [next(it) for _ in range(k)]
+
+    patch, wout, bias, ids, mem, counts, gain, kw, vw, kb, vb = take(11)
+    mem_out, key_out, val_out = take(3)
+    pv, h = take(n), take(n)
+    idsb, oh = take(2)
+    sp, sm, rp, rm, hs = (take(n) for _ in range(5))
+    wv, mv, acc, kvown, wkv, gbuf, mnew, ks, kr = take(9)
+    k1s, k1r, k2s, k2r, sq, kout, vout, ssem, rsem, lsem = take(10)
     seq, mp = lax.axis_index("seq"), lax.axis_index("mp")
     y, z = lax.div(seq, 8), lax.rem(seq, 8)
     x, c = lax.div(mp, 2), lax.rem(mp, 2)
@@ -157,9 +196,9 @@
 
         lax.fori_loop(0, 8, body, 0)
 
-    activate(0)
     got_kw.wait()
     got_vw.wait()
+    activate(0)
     pl.semaphore_wait(barrier, len(partners))
 
     yc = [{} for _ in CHUNKS]
@@ -168,57 +207,72 @@
         yc[i]["p"] = remote(h[i].at[0], h[i].at[1], yp)
         yc[i]["m"] = remote(h[i].at[0], h[i].at[2], ym)
 
-    def y_fwd(i):
-        yc[i]["p"].wait_recv()
-        yc[i]["fp"] = remote(h[i].at[1, pl.ds(0, 256)], h[i].at[3, pl.ds(0, 256)], yp)
-        yc[i]["m"].wait_recv()
-        yc[i]["fm"] = remote(h[i].at[2, pl.ds(256, 256)], h[i].at[3, pl.ds(256, 256)], ym)
-
-    def y_done(i):
-        yc[i]["fp"].wait_recv()
-        yc[i]["fm"].wait_recv()
+    def y_fwd(i, back):
+        if not back:
+            yc[i]["p"].wait_recv()
+            part = pl.ds(0, 256)
+            yc[i]["fp"] = remote(h[i].at[1, part], h[i].at[3, part], yp)
+        else:
+            yc[i]["m"].wait_recv()
+            part = pl.ds(256, 256)
+            yc[i]["fm"] = remote(h[i].at[2, part], h[i].at[3, part], ym)
 
     wc = {}
+    rows_a, rows_b = pl.ds(0, 256 - ROWS_B), pl.ds(256 - ROWS_B, ROWS_B)
+    half_a = [pl.ds(0, 128 - ROWS_B // 2), pl.ds(128 - ROWS_B // 2, 128 - ROWS_B // 2)]
+    half_b = [pl.ds(256 - ROWS_B, ROWS_B // 2), pl.ds(256 - ROWS_B // 2, ROWS_B // 2)]
+    perm_to_z = lax.rem(2 * lax.rem(z, 4) + c + 4, 8)
+
+    def same(where, land, to):
+        return remote(wkv.at[where], wkv.at[where], to, land=wkv.at[land])
+
+    def once(key):
+        copy = wc.pop(key, None)
+        if copy is not None:
+            copy.wait_recv()
 
     def w_perm():
-        wc["perm"] = remote(kvown, wkv.at[perm_to_y, perm_to_z], perm_to, land=wkv.at[y, z])
-
-    perm_to_y = x
-    perm_to_z = lax.rem(2 * lax.rem(z, 4) + c + 4, 8)
-
-    def w_z(t):
+        wc["perm"] = remote(kvown, wkv.at[x, perm_to_z], perm_to, land=wkv.at[y, z])
+
+    def w_z(t, back):
+        once("perm")
+        once(("z", t - 1, back))
+        sign, to = (-1, zm) if back else (1, zp)
+        src, land = m8(z - sign * (t - 1)), m8(z - sign * t)
+        part = rows_a if t <= 3 else half_a[back]
+        wc["z", t, back] = same((y, src, part), (y, land, part), to)
+
+    def w_y(t, back):
+        sign, to = (-1, ym) if back else (1, yp)
         if t == 1:
-            wc["perm"].wait_recv()
-        else:
-            wc["zp", t - 1].wait_recv()
-            wc["zm", t - 1].wait_recv()
-        if t <= 3:
-            a, b = m8(z - t + 1), m8(z + t - 1)
-            wc["zp", t] = remote(wkv.at[y, a], wkv.at[y, a], zp, land=wkv.at[y, m8(z - t)])
-            wc["zm", t] = remote(wkv.at[y, b], wkv.at[y, b], zm, land=wkv.at[y, m8(z + t)])
-        else:
-            a, b, f = m8(z - 3), m8(z + 3), m8(z + 4)
-            lo, hi = pl.ds(0, 128), pl.ds(128, 128)
-            wc["zp", 4] = remote(wkv.at[y, a, lo], wkv.at[y, a, lo], zp, land=wkv.at[y, f, lo])
-            wc["zm", 4] = remote(wkv.at[y, b, hi], wkv.at[y, b, hi], zm, land=wkv.at[y, f, hi])
-
-    def w_y(t):
+            once(("z", 4, 0))
+            once(("z", 4, 1))
+            every = pl.ds(0, 8)
+            wc["y", 1, back] = same((y, every, rows_a), (m4(y - sign), every, rows_a), to)
+        else:
+            once(("y", 1, back))
+            some = pl.ds(4 * back, 4)
+            wc["y", 2, back] = same(
+                (m4(y - sign), some, rows_a), (m4(y - 2 * sign), some, rows_a), to
+            )
+
+    def b_y(t, back):
+        sign, to = (-1, ym) if back else (1, yp)
+        once("perm")
+        once(("b", t - 1, back))
+        part = rows_b if t == 1 else half_b[back]
+        src, land = m4(y - sign * (t - 1)), m4(y - sign * t)
+        wc["b", t, back] = same((src, z, part), (land, z, part), to)
+
+    def b_z(t, back):
+        sign, to = (-1, zm) if back else (1, zp)
         if t == 1:
-            wc["zp", 4].wait_recv()
-            wc["zm", 4].wait_recv()
-            wc["yp"] = remote(wkv.at[y], wkv.at[y], yp, land=wkv.at[m4(y - 1)])
-            wc["ym"] = remote(wkv.at[y], wkv.at[y], ym, land=wkv.at[m4(y + 1)])
-        else:
-            a, b, f = m4(y - 1), m4(y + 1), m4(y + 2)
-            lo, hi = pl.ds(0, 4), pl.ds(4, 4)
-            wc["yp"].wait_recv()
-            wc["fp"] = remote(wkv.at[a, lo], wkv.at[a, lo], yp, land=wkv.at[f, lo])
-            wc["ym"].wait_recv()
-            wc["fm"] = remote(wkv.at[b, hi], wkv.at[b, hi], ym, land=wkv.at[f, hi])
-
-    def w_done():
-        wc["fp"].wait_recv()
-        wc["fm"].wait_recv()
+            once(("b", 2, 0))
+            once(("b", 2, 1))
+        once(("c", t - 1, back))
+        some = pl.ds(0, 4) if t <= 3 else pl.ds(2 * back, 2)
+        src, land = m8(z - sign * (t - 1)), m8(z - sign * t)
+        wc["c", t, back] = same((some, src, rows_b), (some, land, rows_b), to)
 
     ic = {}
 
@@ -230,10 +284,15 @@
         ic["p"].wait_recv()
         ic["f"] = remote(idsb.at[0, 1], idsb.at[0, 3], yp)
 
+    def i_plane():
+        for key in ("m", "f"):
+            copy = ic.pop(key, None)
+            if copy is not None:
+                copy.wait_recv()
+
     def i_z(t):
         if t == 1:
-            ic["m"].wait_recv()
-            ic["f"].wait_recv()
+            i_plane()
             ic["zp", 1] = remote(idsb.at[0], idsb.at[1], zp)
             ic["zm", 1] = remote(idsb.at[0], idsb.at[5], zm)
         else:
@@ -243,11 +302,9 @@
                 ic["zm", t - 1].wait_recv()
                 ic["zm", t] = remote(idsb.at[3 + t], idsb.at[4 + t], zm)
 
-    def i_done():
-        ic["zp", 4].wait_recv()
-        ic["zm", 3].wait_recv()
-
-    def onehot(lo, hi):
+    def onehot(second):
+        i_plane()
+
         def body(k, carry):
             step = lax.div(k + 1, 2)
             zrel = 4 + step * (1 - 2 * lax.rem(k, 2))
@@ -261,11 +318,11 @@
                     oh[k, :, s * 512 + r * 128 : s * 512 + (r + 1) * 128] = hit
             return carry
 
-        lax.fori_loop(lo, hi, body, 0)
-
-    def sums(i, k, n):
+        lax.fori_loop(1 if second else 0, 8 if second else 1, body, 0)
+
+    def sums(i, k, m):
         w = CHUNKS[i][1]
-        left = oh[k : k + n].reshape(n * 256, 2048)
+        left = oh[k : k + m].reshape(m * 256, 2048)
         return jnp.dot(left, h[i][...].reshape(2048, w), preferred_element_type=F32)
 
     rc = [{} for _ in CHUNKS]
@@ -273,6 +330,8 @@
 
     def rs(i, t):
         if t == 0:
+            yc[i]["fp"].wait_recv()
+            yc[i]["fm"].wait_recv()
             p = sums(i, 0, 1).astype(BF16)
             sp[i][0, lo] = p[:128]
             sm[i][0, hi] = p[128:]
@@ -306,104 +365,84 @@
         xc[i][4] = remote(hs[i].at[0], hs[i].at[4], xm)
         xc[i][1] = remote(hs[i].at[0], hs[i].at[1], sib)
 
-    def x_fwd(i):
-        xc[i][2].wait_recv()
-        xc[i]["fp"] = remote(hs[i].at[2, lo], hs[i].at[6, lo], xp)
-        xc[i][3] = remote(hs[i].at[2], hs[i].at[3], sib)
-        xc[i][4].wait_recv()
-        xc[i]["fm"] = remote(hs[i].at[4, hi], hs[i].at[6, hi], xm)
-        xc[i][5] = remote(hs[i].at[4], hs[i].at[5], sib)
+    def x_fwd(i, back):
+        if not back:
+            xc[i][2].wait_recv()
+            xc[i]["fp"] = remote(hs[i].at[2, lo], hs[i].at[6, lo], xp)
+            xc[i][3] = remote(hs[i].at[2], hs[i].at[3], sib)
+        else:
+            xc[i][4].wait_recv()
+            xc[i]["fm"] = remote(hs[i].at[4, hi], hs[i].at[6, hi], xm)
+            xc[i][5] = remote(hs[i].at[4], hs[i].at[5], sib)
 
     def x_last(i):
         xc[i]["fp"].wait_recv()
         xc[i]["fm"].wait_recv()
         xc[i][7] = remote(hs[i].at[6], hs[i].at[7], sib)
 
-    def mm(i, blocks, first=False):
-        off, w = CHUNKS[i]
-        for b in blocks:
-            if b % 2:
-                xc[i][b].wait_recv()
-            xs = m4(x + (0, -1, 1, 2)[b // 2])
-            src = xs * 2 + (1 - c if b % 2 else c)
-            got = jnp.dot(hs[i][b], wv[src, off : off + w, :], preferred_element_type=F32)
-            acc[...] = got if first and b == blocks[0] else acc[...] + got
-
-    w_perm()
-    y_first(0)
-    activate(1)
-    w_z(1)
-    i_first()
-    y_first(1)
-    i_fwd()
-    w_z(2)
-    activate(2)
-    y_fwd(0)
-    y_first(2)
-    w_z(3)
-    i_z(1)
-    onehot(0, 1)
-    onehot(1, 8)
-    y_fwd(1)
-    w_z(4)
-    y_done(0)
-    rs(0, 0)
-    y_fwd(2)
-    w_y(1)
-    y_done(1)
-    rs(1, 0)
-    rs(0, 1)
-    rs(1, 1)
-    rs(0, 2)
-    y_done(2)
-    rs(2, 0)
-    rs(1, 2)
-    rs(2, 1)
-    rs(0, 3)
-    i_z(2)
-    rs(2, 2)
-    rs(1, 3)
-    rs_end(0)
-    got_w.wait()
-    mm(0, (0, 1), first=True)
-    i_z(3)
-    rs(2, 3)
-    w_y(2)
-    rs_end(1)
-    i_z(4)
-    rs_end(2)
-    i_done()
-    own = seq * 256
-
-    def count(p, carry):
-        slot = lax.broadcasted_iota(jnp.int32, (256, 128), 0) + own
-        for s in range(4):
-            block = idsb[p, s]
-            for r in range(4):
-                carry = carry + jnp.where(slot == block[r : r + 1, :], 1.0, 0.0)
-        return carry
-
-    hits = lax.fori_loop(0, 8, count, jnp.zeros((256, 128), F32))
-    arrivals = jnp.broadcast_to(jnp.sum(hits, axis=1, keepdims=True), (256, 128))
-    weight = jnp.transpose(jnp.broadcast_to(counts[...].astype(F32), (128, 256)))
-    share = 1.0 / (weight + arrivals)
-    x_fwd(0)
-    x_fwd(1)
-    mm(1, (2, 3))
-    x_fwd(2)
-    mm(2, (0, 1))
-    mm(2, (2, 3))
-    mm(0, (2, 3))
-    mm(1, (4, 5))
-    mm(2, (4, 5))
-    mm(0, (4, 5))
-    x_last(0)
-    mm(1, (0, 1))
-    x_last(1)
-    x_last(2)
-    mm(0, (6, 7))
-    mm(1, (6, 7))
-    mm(2, (6, 7))
+    def mm(group, pair):
+        chunks = GROUPS[group]
+        for i in chunks:
+            xc[i][2 * pair + 1].wait_recv()
+        off, w = CHUNKS[chunks[0]][0], sum(CHUNKS[i][1] for i in chunks)
+        if not state.get("acc"):
+            got_w.wait()
+        got = None
+        for b in (2 * pair, 2 * pair + 1):
+            src = m4(x + (0, -1, 1, 2)[pair]) * 2 + (1 - c if b % 2 else c)
+            left = jnp.concatenate([hs[i][b] for i in chunks], axis=1)
+            part = jnp.dot(left, wv[src, off : off + w, :], preferred_element_type=F32)
+            got = part if got is None else got + part
+        if state.get("acc"):
+            acc[...] = acc[...] + got
+        else:
+            acc[...] = got
+            state["acc"] = True
+
+    state = {}
+
+    def count():
+        ic["zp", 4].wait_recv()
+        ic["zm", 3].wait_recv()
+        own = seq * 256
+
+        def body(p, carry):
+            slot = lax.broadcasted_iota(jnp.int32, (256, 128), 0) + own
+            for s in range(4):
+                block = idsb[p, s]
+                for r in range(4):
+                    carry = carry + jnp.where(slot == block[r : r + 1, :], 1.0, 0.0)
+            return carry
+
+        hits = lax.fori_loop(0, 8, body, jnp.zeros((256, 128), F32))
+        state["arrivals"] = jnp.broadcast_to(jnp.sum(hits, axis=1, keepdims=True), (256, 128))
+        weight = jnp.transpose(jnp.broadcast_to(counts[...].astype(F32), (128, 256)))
+        state["weight"] = weight
+        state["share"] = 1.0 / (weight + state["arrivals"])
+
+    table = {
+        "act": activate,
+        "y_first": y_first,
+        "y_fwd": y_fwd,
+        "w_perm": w_perm,
+        "w_z": w_z,
+        "w_y": w_y,
+        "b_y": b_y,
+        "b_z": b_z,
+        "i_first": i_first,
+        "i_fwd": i_fwd,
+        "i_z": i_z,
+        "oh": onehot,
+        "rs": rs,
+        "rs_end": rs_end,
+        "x_fwd": x_fwd,
+        "x_last": x_last,
+        "mm": mm,
+        "count": count,
+    }
+    for event, *where in ORDER:
+        table[event](*where)
+    arrivals, weight, share = state["arrivals"], state["weight"], state["share"]
 
     got_mem.wait()
     squares = jnp.zeros((256, 128), F32)
@@ -426,7 +465,8 @@
                 slot = 2 * d + o
                 sqc.append(remote(sq.at[0], sq.at[slot], dev(dx=d, other=o)))
 
-    w_done()
+    for key in list(wc):
+        once(key)
 
     def heads(d, o):
         ys = m4(x + d)

time: 96.7 us -> 91 us (0.941); the launches traced: 95.3 us -> 90.7 us
  Pallas kernels: 94.5 us -> 89.9 us
    pallas_call x1, Pallas kernels: 92.6 us -> 88 us  [on_device(): pl.pallas_call(kernel, out_shape=(jax.ShapeDtypeStruct((256, 1024), BF16)...]
where the time goes in v3:
time: 91 us; the launch traced here: 90.7 us
  Pallas kernels  89.9 us (99%)
    pallas_call x1, Pallas kernels, on_device(): pl.pallas_call(kernel, out_shape=(jax.ShapeDtypeStruct((256, 1024), BF16)...  88 us
    pallas_call x1, Pallas kernels, on_device(): pl.pallas_call(hand_over, out_shape=tuple((jax.ShapeDtypeStruct(m.shape,...  1.9 us

profile of v3, /device:TPU:6, one launch (start us, length us, event | category | flops | bytes accessed | tf_op | source)
XLA Modules:
  0.0 90.7 jit_solution(12057586572604622544)
XLA Ops:
  0.6 88.0 %shard_map.130 = (bf16[256,1024]{1,0:T(8,128)(2,1)}, bf16[256,128]{1,0:T(8,128)(2,1)}, bf16[256,128]{1,0:T(8,128)(2,1)}) custom-call(bf16[512,640]{1,0:T(8,128)(2,1)} %refs_0_.1, bf16[8,640,1024]{2,1,0:T(8,128)(2,1)} %bitcast.7, bf16[8,128]{1,0:T(8,128)(2,1)} %bitcast.8, s32[4,128]{1,0:T(4,128)} %bitcast.9, bf16[256,1024]{1,0:T(8,128)(2,1)} %refs_4_.1, ...), custom_call_target="tpu_custom_call" | custom-call | flops 10000000000 | bytes 20000000 | tf_op jit(solution)/shard_map/pallas_call | solution.py:575
  88.7 1.9 %shard_map.131 = (bf16[256,1024]{1,0:T(8,128)(2,1)}, bf16[256,128]{1,0:T(8,128)(2,1)}, bf16[256,128]{1,0:T(8,128)(2,1)}) custom-call(bf16[256,1024]{1,0:T(8,128)(2,1)} %get-tuple-element.6.a, bf16[256,128]{1,0:T(8,128)(2,1)} %get-tuple-element.7.b, bf16[256,128]{1,0:T(8,128)(2,1)} %get-tuple-element.8.c), custom_call_target="tpu_custom_call" | custom-call | tf_op jit(solution)/shard_map/pallas_call | solution.py:604

commit v4 on v3

--- a/solution.py
+++ b/solution.py
@@ -6,8 +6,8 @@
 from jax.sharding import PartitionSpec as P
 
 D = 8192
-CHUNKS = ((0, 256), (256, 256), (512, 128))
-GROUPS = ((0,), (1,), (2,))
+CHUNKS = ((0, 128), (128, 128), (256, 128), (384, 128), (512, 128))
+GROUPS = ((0, 1), (2, 3), (4,))
 ROWS_B = 32
 MESH = pl.DeviceIdType.MESH
 N_REMOTE = 160
@@ -16,86 +16,110 @@
 
 ORDER = (
     ("w_perm",),
+    ("y_first", 0),
+    ("act", 2),
     ("i_first",),
-    ("y_first", 0),
+    ("act", 1),
+    ("y_first", 1),
+    ("w_z", 1, 0),
+    ("w_z", 1, 1),
     ("i_fwd",),
-    ("act", 1),
-    ("w_z", 1, 0),
-    ("y_first", 1),
-    ("w_z", 1, 1),
-    ("oh", 0),
-    ("y_fwd", 0, 1),
-    ("i_z", 1),
+    ("y_first", 2),
+    ("act", 4),
+    ("w_z", 2, 0),
+    ("y_fwd", 1, 1),
+    ("y_fwd", 1, 0),
     ("w_z", 2, 1),
     ("y_fwd", 0, 0),
-    ("w_z", 2, 0),
+    ("oh", 0),
+    ("act", 3),
+    ("y_fwd", 0, 1),
+    ("y_first", 3),
     ("oh", 1),
-    ("act", 2),
+    ("rs", 1, 0),
+    ("b_y", 1, 1),
+    ("w_z", 3, 0),
+    ("w_z", 3, 1),
+    ("rs", 0, 0),
+    ("y_first", 4),
+    ("rs", 1, 1),
+    ("b_y", 1, 0),
+    ("y_fwd", 3, 0),
+    ("b_y", 2, 1),
+    ("y_fwd", 2, 0),
+    ("i_z", 1),
+    ("y_fwd", 3, 1),
+    ("w_z", 4, 0),
+    ("w_z", 4, 1),
+    ("y_fwd", 2, 1),
+    ("rs", 0, 1),
+    ("y_fwd", 4, 0),
+    ("y_fwd", 4, 1),
+    ("rs", 1, 2),
+    ("b_y", 2, 0),
     ("i_z", 2),
-    ("w_z", 3, 0),
-    ("y_fwd", 1, 1),
-    ("y_fwd", 1, 0),
-    ("w_z", 3, 1),
-    ("y_first", 2),
-    ("rs", 0, 0),
-    ("w_z", 4, 0),
-    ("i_z", 3),
-    ("w_z", 4, 1),
-    ("b_y", 1, 1),
-    ("rs", 1, 0),
-    ("b_y", 1, 0),
-    ("rs", 0, 1),
-    ("y_fwd", 2, 1),
-    ("y_fwd", 2, 0),
-    ("i_z", 4),
-    ("b_y", 2, 0),
+    ("rs", 3, 0),
     ("w_y", 1, 0),
-    ("b_y", 2, 1),
     ("w_y", 1, 1),
-    ("rs", 1, 1),
     ("rs", 2, 0),
     ("rs", 0, 2),
+    ("rs", 4, 0),
+    ("rs", 1, 3),
+    ("rs", 3, 1),
+    ("i_z", 3),
+    ("rs", 4, 1),
+    ("rs", 0, 3),
+    ("rs_end", 1),
     ("rs", 2, 1),
-    ("rs", 1, 2),
-    ("rs", 0, 3),
+    ("rs", 4, 2),
+    ("rs", 3, 2),
+    ("x_fwd", 1, 0),
+    ("i_z", 4),
+    ("rs_end", 0),
     ("rs", 2, 2),
-    ("rs", 1, 3),
+    ("rs", 4, 3),
     ("b_z", 1, 1),
-    ("count",),
     ("b_z", 1, 0),
-    ("rs_end", 0),
+    ("rs", 3, 3),
     ("rs", 2, 3),
-    ("rs_end", 1),
-    ("b_z", 2, 1),
-    ("w_y", 2, 1),
-    ("w_y", 2, 0),
+    ("rs_end", 4),
+    ("mm", 0, 0),
     ("b_z", 2, 0),
-    ("rs_end", 2),
     ("x_fwd", 0, 0),
     ("x_fwd", 0, 1),
+    ("w_y", 2, 0),
+    ("w_y", 2, 1),
     ("x_fwd", 1, 1),
-    ("x_fwd", 1, 0),
+    ("b_z", 2, 1),
+    ("rs_end", 3),
+    ("mm", 2, 0),
+    ("rs_end", 2),
+    ("x_fwd", 4, 1),
+    ("x_last", 0),
+    ("x_fwd", 4, 0),
+    ("b_z", 3, 0),
+    ("b_z", 3, 1),
+    ("mm", 2, 2),
+    ("x_fwd", 3, 1),
+    ("x_fwd", 3, 0),
+    ("count",),
+    ("x_last", 1),
+    ("x_fwd", 2, 0),
+    ("mm", 2, 1),
+    ("x_fwd", 2, 1),
+    ("x_last", 4),
+    ("mm", 0, 2),
+    ("mm", 1, 2),
+    ("mm", 2, 3),
+    ("mm", 1, 1),
+    ("b_z", 4, 0),
+    ("b_z", 4, 1),
     ("mm", 0, 1),
-    ("mm", 0, 0),
-    ("b_z", 3, 0),
-    ("mm", 0, 2),
-    ("b_z", 3, 1),
-    ("x_fwd", 2, 1),
-    ("mm", 1, 2),
-    ("mm", 1, 1),
-    ("mm", 2, 0),
-    ("x_fwd", 2, 0),
-    ("mm", 2, 2),
     ("mm", 1, 0),
-    ("x_last", 0),
-    ("b_z", 4, 0),
-    ("x_last", 1),
+    ("x_last", 3),
     ("mm", 0, 3),
-    ("b_z", 4, 1),
+    ("x_last", 2),
     ("mm", 1, 3),
-    ("x_last", 2),
-    ("mm", 2, 1),
-    ("mm", 2, 3),
 )
 
 
@@ -196,9 +220,9 @@
 
         lax.fori_loop(0, 8, body, 0)
 
+    activate(0)
     got_kw.wait()
     got_vw.wait()
-    activate(0)
     pl.semaphore_wait(barrier, len(partners))
 
     yc = [{} for _ in CHUNKS]
@@ -456,14 +480,16 @@
         squares = squares + stored * stored
         gbuf[:, col] = (stored * gain[j : j + 1, :].astype(F32)).astype(BF16)
     put_mem = local(mnew, mem_out)
-    mine = jnp.broadcast_to(jnp.sum(squares, axis=1, keepdims=True), (256, 128))
-    sq[0] = jnp.transpose(mine)[:8, :]
     sqc = []
-    for d in (0, 1, 2, 3):
-        for o in (False, True):
-            if d or o:
-                slot = 2 * d + o
-                sqc.append(remote(sq.at[0], sq.at[slot], dev(dx=d, other=o)))
+
+    def share_squares():
+        mine = jnp.broadcast_to(jnp.sum(squares, axis=1, keepdims=True), (256, 128))
+        sq[0] = jnp.transpose(mine)[:8, :]
+        for d in (0, 1, 2, 3):
+            for o in (False, True):
+                if d or o:
+                    slot = 2 * d + o
+                    sqc.append(remote(sq.at[0], sq.at[slot], dev(dx=d, other=o)))
 
     for key in list(wc):
         once(key)
@@ -481,15 +507,21 @@
         return total
 
     kc = {}
-    for d in (2, 1, 3, 0):
+
+    def give(d):
         ks[d] = heads(d, True).astype(BF16)
         kc[d] = remote(ks.at[d], kr.at[d], sib)
+
+    give(2)
     p = heads(2, False)
+    give(1)
     kc[2].wait_recv()
-    p = (p + kr[2].astype(F32)).astype(BF16)
-    k1s[...] = p
+    k1s[...] = (p + kr[2].astype(F32)).astype(BF16)
     kc["p1"] = remote(k1s.at[lo], k1r.at[lo], xp)
     kc["m1"] = remote(k1s.at[hi], k1r.at[hi], xm)
+    give(3)
+    share_squares()
+    give(0)
     for d, half, key, to in ((1, 0, "p", xp), (3, 1, "m", xm)):
         p = heads(d, False)
         kc[d].wait_recv()

time: 91 us -> 90.7 us (level)
  no operation moved by 1% of the time
where the time goes in v4:
time: 90.7 us; the launch traced here: 90.5 us
  Pallas kernels  89.7 us (99%)
    pallas_call x1, Pallas kernels, on_device(): pl.pallas_call(kernel, out_shape=(jax.ShapeDtypeStruct((256, 1024), BF16)...  87.8 us
    pallas_call x1, Pallas kernels, on_device(): pl.pallas_call(hand_over, out_shape=tuple((jax.ShapeDtypeStruct(m.shape,...  1.9 us

profile of v4, /device:TPU:6, one launch (start us, length us, event | category | flops | bytes accessed | tf_op | source)
XLA Modules:
  0.0 90.5 jit_solution(14481076750616655469)
XLA Ops:
  0.6 87.8 %shard_map.130 = (bf16[256,1024]{1,0:T(8,128)(2,1)}, bf16[256,128]{1,0:T(8,128)(2,1)}, bf16[256,128]{1,0:T(8,128)(2,1)}) custom-call(bf16[512,640]{1,0:T(8,128)(2,1)} %refs_0_.1, bf16[8,640,1024]{2,1,0:T(8,128)(2,1)} %bitcast.7, bf16[8,128]{1,0:T(8,128)(2,1)} %bitcast.8, s32[4,128]{1,0:T(4,128)} %bitcast.9, bf16[256,1024]{1,0:T(8,128)(2,1)} %refs_4_.1, ...), custom_call_target="tpu_custom_call" | custom-call | flops 10000000000 | bytes 20000000 | tf_op jit(solution)/shard_map/pallas_call | solution.py:607
  88.5 1.9 %shard_map.131 = (bf16[256,1024]{1,0:T(8,128)(2,1)}, bf16[256,128]{1,0:T(8,128)(2,1)}, bf16[256,128]{1,0:T(8,128)(2,1)}) custom-call(bf16[256,1024]{1,0:T(8,128)(2,1)} %get-tuple-element.6.a, bf16[256,128]{1,0:T(8,128)(2,1)} %get-tuple-element.7.b, bf16[256,128]{1,0:T(8,128)(2,1)} %get-tuple-element.8.c), custom_call_target="tpu_custom_call" | custom-call | tf_op jit(solution)/shard_map/pallas_call | solution.py:636

commit v5 on v4

--- a/solution.py
+++ b/solution.py
@@ -197,7 +197,7 @@
         return copy
 
     barrier = pltpu.get_barrier_semaphore()
-    partners = [yp, ym, zp, zm, perm_to, perm_from, sib]
+    partners = [perm_to, perm_from, yp, ym, zp, zm, sib]
     partners += [dev(dx=d, other=o) for d in (1, 2, 3) for o in (False, True)]
     for partner in partners:
         pl.semaphore_signal(barrier, inc=1, device_id=partner, device_id_type=MESH)
@@ -205,8 +205,6 @@
     got_patch = [local(patch.at[:, pl.ds(o, w)], pv[i]) for i, (o, w) in enumerate(CHUNKS)]
     got_kw = local(kw, kvown.at[:, pl.ds(0, 128)])
     got_vw = local(vw, kvown.at[:, pl.ds(128, 128)])
-    got_mem = local(mem, mv)
-    got_w = local(wout, wv)
 
     idsb[0, 0] = ids[...]
 
@@ -224,6 +222,8 @@
     got_kw.wait()
     got_vw.wait()
     pl.semaphore_wait(barrier, len(partners))
+    got_w = local(wout, wv)
+    got_mem = local(mem, mv)
 
     yc = [{} for _ in CHUNKS]
 

time: 90.7 us -> 90.6 us (level)
  no operation moved by 1% of the time
where the time goes in v5:
time: 90.6 us; the launch traced here: 90.5 us
  Pallas kernels  89.7 us (99%)
    pallas_call x1, Pallas kernels, on_device(): pl.pallas_call(kernel, out_shape=(jax.ShapeDtypeStruct((256, 1024), BF16)...  87.8 us
    pallas_call x1, Pallas kernels, on_device(): pl.pallas_call(hand_over, out_shape=tuple((jax.ShapeDtypeStruct(m.shape,...  1.9 us

profile of v5, /device:TPU:6, one launch (start us, length us, event | category | flops | bytes accessed | tf_op | source)
XLA Modules:
  0.0 90.5 jit_solution(1648874540923522255)
XLA Ops:
  0.6 87.8 %shard_map.130 = (bf16[256,1024]{1,0:T(8,128)(2,1)}, bf16[256,128]{1,0:T(8,128)(2,1)}, bf16[256,128]{1,0:T(8,128)(2,1)}) custom-call(bf16[512,640]{1,0:T(8,128)(2,1)} %refs_0_.1, bf16[8,640,1024]{2,1,0:T(8,128)(2,1)} %bitcast.7, bf16[8,128]{1,0:T(8,128)(2,1)} %bitcast.8, s32[4,128]{1,0:T(4,128)} %bitcast.9, bf16[256,1024]{1,0:T(8,128)(2,1)} %refs_4_.1, ...), custom_call_target="tpu_custom_call" | custom-call | flops 10000000000 | bytes 20000000 | tf_op jit(solution)/shard_map/pallas_call | solution.py:607
  88.4 1.9 %shard_map.131 = (bf16[256,1024]{1,0:T(8,128)(2,1)}, bf16[256,128]{1,0:T(8,128)(2,1)}, bf16[256,128]{1,0:T(8,128)(2,1)}) custom-call(bf16[256,1024]{1,0:T(8,128)(2,1)} %get-tuple-element.6.a, bf16[256,128]{1,0:T(8,128)(2,1)} %get-tuple-element.7.b, bf16[256,128]{1,0:T(8,128)(2,1)} %get-tuple-element.8.c), custom_call_target="tpu_custom_call" | custom-call | tf_op jit(solution)/shard_map/pallas_call | solution.py:636
